TPU v7x, 128 devices: a whole 4x4x4 slice. The times are simulated.
128 devices in a mesh: dp: 8 (over y_lo, x), seq: 8 (over z, core), branch: 2 (over y_hi).
Axes of the slice: x: 4, y: 4 (y_hi: 2, y_lo: 2; y = y_hi * 2 + y_lo), z: 4, core: 2. Of those that a mesh axis runs over, the one named last changes fastest.
Arguments:
- inputs: bfloat16 [8, 2048, 2048], P('dp', ('seq', 'branch')), may hold values from -6 to 6
- segment_ids: int32 [8, 2048], P('dp'), may hold values from 0 to 4, as said below
- valid_mask: int32 [8, 2048], P('dp'), may hold values from 0 to 1, as said below
- norm_gain: bfloat16 [2048], replicated, may hold values from 0.5 to 1.5
- norm_bias: bfloat16 [2048], replicated, may hold values from -2 to 2
- qkv_weight: bfloat16 [2048, 3, 2048], P(('dp', 'seq'), None, 'branch'), may hold values from -0.125 to 0.125
- qkv_bias: bfloat16 [3, 2048], P(None, 'branch'), may hold values from -3 to 3
- attn_out_weight: bfloat16 [2048, 2048], P(('dp', 'seq'), 'branch'), may hold values from -0.75 to 0.75
- up_weight: bfloat16 [2048, 8192], P(('dp', 'seq'), 'branch'), may hold values from -0.125 to 0.125
- up_bias: bfloat16 [8192], P('branch'), may hold values from -3 to 3
- down_weight: bfloat16 [2048, 8192], P(('dp', 'seq'), 'branch'), may hold values from -0.0625 to 0.0625
- out_bias: bfloat16 [2048], replicated, may hold values from -3 to 3
- grad_out: bfloat16 [8, 2048, 2048], P('dp', ('seq', 'branch')), may hold values from -6 to 6
Outputs:
- output: bfloat16 [8, 2048, 2048], P('dp', ('seq', 'branch'))
- grad_inputs: float32 [8, 2048, 2048], P('dp', ('seq', 'branch'))
- grad_norm_gain: float32 [2048], replicated
- grad_norm_bias: float32 [2048], replicated
- grad_qkv_weight: float32 [2048, 3, 2048], P(('dp', 'seq'), None, 'branch')
- grad_qkv_bias: float32 [3, 2048], P(None, 'branch')
- grad_attn_out_weight: float32 [2048, 2048], P(('dp', 'seq'), 'branch')
- grad_up_weight: float32 [2048, 8192], P(('dp', 'seq'), 'branch')
- grad_up_bias: float32 [8192], P('branch')
- grad_down_weight: float32 [2048, 8192], P(('dp', 'seq'), 'branch')
- grad_out_bias: float32 [2048], replicated
Inputs may be any that keep to these rules, and one draw needn't show every extreme that they name: `segment_ids`: within a row the ids never fall and each of the documents 0 to 4 is present; padding tokens carry the id of the last document. `valid_mask`: 0 exactly on a run of padding of two tokens or more at the end of each row.
All inputs are finite; a program needn't handle non-finite values.
Results may differ from a plain program's by a relative error of at most 0.013.
Values may be sent and summed in bfloat16 or wider, within the bound.
A program may use at most 256 MiB of HBM per device.

v0:
```python
import jax
import jax.numpy as jnp
from jax import lax
from jax.sharding import PartitionSpec as P

HD = 64
ROT = 32


EPSILON = 1e-05
MASKED = -1e30


def gelu_tanh(value):
    return (
        0.5
        * value
        * (1.0 + jnp.tanh(0.7978845608028654 * (value + 0.044715 * value * value * value)))
    )


def layer_norm(widened, gain, shift):
    mean = jnp.mean(widened, -1, keepdims=True)
    centred = widened - mean
    variance = jnp.mean(centred * centred, -1, keepdims=True)
    return centred * lax.rsqrt(variance + EPSILON) * gain + shift


def positions_of(segment):
    index = jnp.arange(segment.shape[-1], dtype=jnp.int32)
    before = jnp.concatenate([segment[..., :1] - 1, segment[..., :-1]], -1)
    starts = jnp.where(segment != before, index, 0)
    return index - lax.cummax(starts, axis=segment.ndim - 1)


def rotary(value, place, sign):
    half = ROT // 2
    rates = 10000.0 ** (-2.0 * jnp.arange(half, dtype=jnp.float32) / ROT)
    angle = place.astype(jnp.float32)[..., None] * rates
    cosine = jnp.cos(angle)[..., None, :]
    sine = sign * jnp.sin(angle)[..., None, :]
    first = value[..., :half]
    second = value[..., half:ROT]
    return jnp.concatenate(
        [first * cosine - second * sine, second * cosine + first * sine, value[..., ROT:]], -1
    )


def allowed_mask(seg_query, index_query, seg_key, index_key, valid_key):
    same = seg_query[..., :, None] == seg_key[..., None, :]
    causal = index_key[None, :] <= index_query[:, None]
    live = valid_key[..., None, :] == 1
    itself = index_key[None, :] == index_query[:, None]
    return same & causal & live | itself


def to_blocks(array, block):
    shaped = array.reshape((array.shape[0], array.shape[1] // block, block) + array.shape[2:])
    return jnp.moveaxis(shaped, 1, 0)


def from_blocks(array):
    shaped = jnp.moveaxis(array, 0, 1)
    return shaped.reshape((shaped.shape[0], shaped.shape[1] * shaped.shape[2]) + shaped.shape[3:])


def split_heads(array):
    return array.reshape(array.shape[:-1] + (array.shape[-1] // HD, HD))


def shards(
    inputs,
    segment_ids,
    valid_mask,
    norm_gain,
    norm_bias,
    qkv_weight,
    qkv_bias,
    attn_out_weight,
    up_weight,
    up_bias,
    down_weight,
    out_bias,
    grad_out,
):
    row_count = inputs.shape[0]
    shard_rows = qkv_weight.shape[0]
    head_width = qkv_weight.shape[2]
    head_count = head_width // HD
    length = segment_ids.shape[1]
    seq_tokens = length // lax.axis_size("seq")
    block = min(512, length)
    first_token = lax.axis_index("seq") * seq_tokens
    scale = HD ** (-0.5)
    widened = inputs.astype(jnp.float32)
    gain = norm_gain.astype(jnp.float32)
    shift = norm_bias.astype(jnp.float32)
    normed = layer_norm(widened, gain, shift).astype(jnp.bfloat16)
    normed_all, grad_all = (
        lax.all_gather(normed, "branch", axis=1, tiled=True),
        lax.all_gather(grad_out, "branch", axis=1, tiled=True),
    )
    weights_in = jnp.concatenate([qkv_weight.reshape(shard_rows, 3 * head_width), up_weight], 1)
    weights_out = jnp.concatenate([attn_out_weight, down_weight], 1)
    columns = normed_all
    entry = jnp.einsum(
        "rtd,dc->rtc",
        columns,
        lax.all_gather(weights_in, ("dp", "seq"), axis=0, tiled=True),
        preferred_element_type=jnp.float32,
    )
    triple = entry[..., : 3 * head_width].reshape(
        row_count, seq_tokens, 3, head_width
    ) + qkv_bias.astype(jnp.float32)
    hidden = entry[..., 3 * head_width :] + up_bias.astype(jnp.float32)
    place = positions_of(segment_ids)
    own_place = lax.dynamic_slice_in_dim(place, first_token, seq_tokens, 1)
    own_segment = lax.dynamic_slice_in_dim(segment_ids, first_token, seq_tokens, 1)
    own_index = first_token + jnp.arange(seq_tokens, dtype=jnp.int32)
    query = rotary(split_heads(triple[:, :, 0]), own_place, 1.0).astype(jnp.bfloat16)
    key = rotary(split_heads(triple[:, :, 1]), own_place, 1.0).astype(jnp.bfloat16)
    value = triple[:, :, 2].astype(jnp.bfloat16)
    key_all, value_all = (
        lax.all_gather(key.reshape(row_count, seq_tokens, head_width), "seq", axis=1, tiled=True),
        lax.all_gather(value, "seq", axis=1, tiled=True),
    )
    index_blocks = jnp.arange(length, dtype=jnp.int32).reshape(length // block, block)
    key_items = (
        to_blocks(key_all, block),
        to_blocks(value_all, block),
        to_blocks(segment_ids, block),
        to_blocks(valid_mask, block),
        index_blocks,
    )

    def scores_of(query_heads, key_heads, mask):
        scores = (
            jnp.einsum(
                "rqhd,rkhd->rhqk", query_heads, key_heads, preferred_element_type=jnp.float32
            )
            * scale
        )
        return jnp.where(mask[:, None], scores, MASKED)

    def forward_step(carry, item):
        running, normaliser, weighted = carry
        key_block, value_block, segment_block, valid_block, index_block = item
        scores = scores_of(
            query,
            split_heads(key_block),
            allowed_mask(own_segment, own_index, segment_block, index_block, valid_block),
        )
        newest = jnp.maximum(running, jnp.max(scores, -1))
        fade = jnp.exp(running - newest)
        probability = jnp.exp(scores - newest[..., None])
        normaliser = normaliser * fade + jnp.sum(probability, -1)
        weighted = weighted * fade[..., None] + jnp.einsum(
            "rhqk,rkhd->rhqd",
            probability.astype(jnp.bfloat16),
            split_heads(value_block),
            preferred_element_type=jnp.float32,
        )
        return ((newest, normaliser, weighted), None)

    stats_shape = (row_count, head_count, seq_tokens)
    start_carry = (
        jnp.full(stats_shape, MASKED, jnp.float32),
        jnp.zeros(stats_shape, jnp.float32),
        jnp.zeros(stats_shape + (HD,), jnp.float32),
    )
    (running, normaliser, weighted), unused = lax.scan(forward_step, start_carry, key_items)
    log_total = running + jnp.log(normaliser)
    attended = weighted / normaliser[..., None]
    heads_out = jnp.transpose(attended, (0, 2, 1, 3)).reshape(row_count, seq_tokens, head_width)
    activated = gelu_tanh(hidden).astype(jnp.bfloat16)
    joined = jnp.concatenate([heads_out.astype(jnp.bfloat16), activated], -1)
    branch_part = jnp.einsum(
        "rtc,nc->rtn",
        joined,
        lax.all_gather(weights_out, ("dp", "seq"), axis=0, tiled=True),
        preferred_element_type=jnp.float32,
    )
    columns = grad_all
    back = jnp.einsum(
        "rtn,nc->rtc",
        columns,
        lax.all_gather(weights_out, ("dp", "seq"), axis=0, tiled=True),
        preferred_element_type=jnp.float32,
    )
    grad_heads = back[..., :head_width].astype(jnp.bfloat16)
    unused, gelu_pull = jax.vjp(gelu_tanh, hidden)
    grad_hidden = gelu_pull(back[..., head_width:])[0].astype(jnp.bfloat16)
    columns = grad_all
    grad_weights_out = lax.psum_scatter(
        jnp.einsum("rtn,rtc->nc", columns, joined, preferred_element_type=jnp.float32),
        ("dp", "seq"),
        scatter_dimension=0,
        tiled=True,
    )
    grad_split = split_heads(grad_heads)
    delta = jnp.sum(
        jnp.transpose(split_heads(grad_heads.astype(jnp.float32)), (0, 2, 1, 3)) * attended, -1
    )

    def key_step(grad_query, item):
        key_block, value_block, segment_block, valid_block, index_block = item
        key_heads = split_heads(key_block)
        scores = scores_of(
            query,
            key_heads,
            allowed_mask(own_segment, own_index, segment_block, index_block, valid_block),
        )
        probability = jnp.exp(scores - log_total[..., None])
        grad_prob = jnp.einsum(
            "rqhd,rkhd->rhqk",
            grad_split,
            split_heads(value_block),
            preferred_element_type=jnp.float32,
        )
        grad_score = (probability * (grad_prob - delta[..., None])).astype(jnp.bfloat16)
        grad_query = grad_query + jnp.einsum(
            "rhqk,rkhd->rqhd", grad_score, key_heads, preferred_element_type=jnp.float32
        )
        grad_key = jnp.einsum(
            "rhqk,rqhd->rkhd", grad_score, query, preferred_element_type=jnp.float32
        )
        grad_value = jnp.einsum(
            "rhqk,rqhd->rkhd",
            probability.astype(jnp.bfloat16),
            grad_split,
            preferred_element_type=jnp.float32,
        )
        return (
            grad_query,
            (
                grad_key.reshape(row_count, block, head_width),
                grad_value.reshape(row_count, block, head_width),
            ),
        )

    grad_query, (key_terms, value_terms) = lax.scan(
        key_step, jnp.zeros((row_count, seq_tokens, head_count, HD), jnp.float32), key_items
    )
    grad_key, grad_value = (
        lax.psum_scatter(
            from_blocks(key_terms).astype(jnp.bfloat16), "seq", scatter_dimension=1, tiled=True
        ).astype(jnp.float32),
        lax.psum_scatter(
            from_blocks(value_terms).astype(jnp.bfloat16), "seq", scatter_dimension=1, tiled=True
        ).astype(jnp.float32),
    )
    grad_query = rotary(grad_query * scale, own_place, -1.0).reshape(
        row_count, seq_tokens, head_width
    )
    grad_key = rotary(split_heads(grad_key) * scale, own_place, -1.0).reshape(
        row_count, seq_tokens, head_width
    )
    grad_triple = jnp.concatenate([grad_query, grad_key, grad_value], -1).astype(jnp.bfloat16)
    grad_entry = jnp.concatenate([grad_triple, grad_hidden], -1)
    grad_normed_part = jnp.einsum(
        "rtc,nc->rtn",
        grad_entry,
        lax.all_gather(weights_in, ("dp", "seq"), axis=0, tiled=True),
        preferred_element_type=jnp.float32,
    )
    columns = normed_all
    grad_weights_in = lax.psum_scatter(
        jnp.einsum("rtn,rtc->nc", columns, grad_entry, preferred_element_type=jnp.float32),
        ("dp", "seq"),
        scatter_dimension=0,
        tiled=True,
    )
    out_sum, grad_normed = (
        lax.psum_scatter(
            branch_part.astype(jnp.bfloat16), "branch", scatter_dimension=1, tiled=True
        ).astype(jnp.float32),
        lax.psum_scatter(
            grad_normed_part.astype(jnp.bfloat16), "branch", scatter_dimension=1, tiled=True
        ).astype(jnp.float32),
    )
    output = (widened + out_sum + out_bias.astype(jnp.float32)).astype(jnp.bfloat16)
    unused, norm_pull = jax.vjp(layer_norm, widened, gain, shift)
    grad_widened, grad_gain, grad_shift = norm_pull(grad_normed)
    grad_inputs = grad_widened + grad_out.astype(jnp.float32)
    slots = (
        jnp.arange(lax.axis_size("branch"), dtype=jnp.int32) == lax.axis_index("branch")
    ).astype(jnp.float32)
    bias_terms = jnp.sum(grad_entry.astype(jnp.float32), (0, 1))
    slot_terms = slots[:, None] * bias_terms[None, :]
    out_bias_terms = jnp.sum(grad_out.astype(jnp.float32), (0, 1))
    slot_sum, grad_norm_gain, grad_norm_bias, grad_out_bias = lax.psum(
        (slot_terms, grad_gain, grad_shift, out_bias_terms), ("dp", "seq", "branch")
    )
    own_bias = jnp.sum(slots[:, None] * slot_sum, 0)
    grad_qkv_weight = grad_weights_in[:, : 3 * head_width].reshape(shard_rows, 3, head_width)
    grad_up_weight = grad_weights_in[:, 3 * head_width :]
    grad_attn_out_weight = grad_weights_out[:, :head_width]
    grad_down_weight = grad_weights_out[:, head_width:]
    grad_qkv_bias = own_bias[: 3 * head_width].reshape(3, head_width)
    grad_up_bias = own_bias[3 * head_width :]
    return (
        output,
        grad_inputs,
        grad_norm_gain,
        grad_norm_bias,
        grad_qkv_weight,
        grad_qkv_bias,
        grad_attn_out_weight,
        grad_up_weight,
        grad_up_bias,
        grad_down_weight,
        grad_out_bias,
    )


def solution(mesh):
    placed = (
        P("dp", ("seq", "branch"), None),
        P("dp", None),
        P("dp", None),
        P(),
        P(),
        P(("dp", "seq"), None, "branch"),
        P(None, "branch"),
        P(("dp", "seq"), "branch"),
        P(("dp", "seq"), "branch"),
        P("branch"),
        P(("dp", "seq"), "branch"),
        P(),
        P("dp", ("seq", "branch"), None),
    )
    return jax.shard_map(
        shards,
        mesh=mesh,
        in_specs=placed,
        out_specs=(
            P("dp", ("seq", "branch"), None),
            P("dp", ("seq", "branch"), None),
            P(),
            P(),
            P(("dp", "seq"), None, "branch"),
            P(None, "branch"),
            P(("dp", "seq"), "branch"),
            P(("dp", "seq"), "branch"),
            P("branch"),
            P(("dp", "seq"), "branch"),
            P(),
        ),
        check_vma=False,
    )
```

profile of v0, /device:TPU:24, one launch (start us, length us, event | category | flops | bytes accessed | tf_op | source)
XLA Modules:
  0.0 1601.1 jit_solution(3973087891760334008)
XLA Ops:
  18.5 21.6 %all-gather.8.cloned.1.call-done = bf16[1,256,2048]{2,1,0:T(8,128)(2,1)} async-done(((bf16[1,128,2048]{2,1,0:T(8,128)(2,1)}), bf16[1,256,2048]{2,1,0:T(8,128)(2,1)}) %all-gather.8.cloned.1.call-update) | async-done | bytes 1048592 | tf_op jit(solution)/shard_map/all_gather | solution.py:100
  40.1 168.7 %all-gather.10.cloned.1.call-done = bf16[2048,7168]{1,0:T(8,128)(2,1)} async-done(((bf16[32,7168]{1,0:T(8,128)(2,1)}), bf16[2048,7168]{1,0:T(8,128)(2,1)}) %all-gather.10.cloned.1.call-update) | async-done | bytes 29360144 | tf_op jit(solution)/shard_map/all_gather | solution.py:109
  208.8 13.6 convolution_bitcast_fusion.2
  222.4 2.9 copy-done.2
  239.0 128.8 %all-gather.14.cloned.1.call-done = bf16[2048,5120]{1,0:T(8,128)(2,1)} async-done(((bf16[32,5120]{1,0:T(8,128)(2,1)}), bf16[2048,5120]{1,0:T(8,128)(2,1)}) %all-gather.14.cloned.1.call-update) | async-done | bytes 20971536 | tf_op jit(solution)/shard_map/all_gather | solution.py:180
  367.8 10.1 convolution_bitcast_fusion.3
  380.6 25.1 %all-gather.18.cloned.1.call-done = bf16[1,2048,1,1024]{1,3,2,0:T(8,128)(2,1)} async-done(((bf16[1,256,1,1024]{1,3,2,0:T(8,128)(2,1)}), bf16[1,2048,1,1024]{1,3,2,0:T(8,128)(2,1)}) %all-gather.18.cloned.1.call-update) | async-done | bytes 4194320 | tf_op jit(solution)/shard_map/all_gather | solution.py:125
  405.7 6.3 copy.125
  412.0 6.2 copy.127
  418.2 26.7 %all-gather.12.cloned.1.call-done = bf16[1,2048,1024]{1,2,0:T(8,128)(2,1)} async-done(((bf16[1,256,1024]{1,2,0:T(8,128)(2,1)}), bf16[1,2048,1024]{1,2,0:T(8,128)(2,1)}) %all-gather.12.cloned.1.call-update) | async-done | bytes 4194320 | tf_op jit(solution)/shard_map/all_gather | solution.py:124
  445.0 6.3 copy.124
  451.3 6.3 copy.126
  457.6 30.3 %while.30 = (s32[]{:T(128)}, f32[1,16,256]{2,1,0:T(8,128)S(1)}, f32[1,16,256]{2,1,0:T(8,128)S(1)}, f32[1,16,256,64]{2,3,1,0:T(8,128)S(1)}, s32[1,256]{1,0:T(1,12...) while((s32[]{:T(128)}, f32[1,16,256]{2,1,0:T(8,128)S(1)}, ...), condition=%wide.region_7.8_spmd.clone, body=%wide.region_4.7_spmd.clone.sunk | while | flops 561537792 | bytes 34883756 | solution.py:171
  488.9 63.6 %while.31 = (s32[]{:T(128)}, f32[1,256,16,64]{1,3,2,0:T(8,128)}, bf16[4,1,512,1024]{3,2,0,1:T(8,128)(2,1)}, bf16[4,1,512,1024]{2,3,1,0:T(8,128)(2,1)}, bf16[4,1,...) while((s32[]{:T(128)}, f32[1,256,16,64]{1,3,2,0:T(8,128)}, ...), condition=%wide.region_11.12_spmd.clone, body=%wide.region_10.11_spmd.clone.sunk | while | flops 1364460288 | bytes 58132680 | solution.py:241
  514.2 3.0 fusion.132
  530.3 3.0 fusion.132
  546.5 3.0 fusion.132
  552.6 6.3 copy.135
  560.7 7.7 fusion.43
  571.8 19.9 %reduce-scatter.11.cloned.1.call-done = bf16[1,256,1024]{2,1,0:T(8,128)(2,1)} async-done(((bf16[1,2048,1024]{2,1,0:T(8,128)(2,1)}), bf16[1,256,1024]{2,1,0:T(8,128)(2,1)}) %reduce-scatter.11.cloned.1.call-update) | async-done | bytes 524304 | tf_op jit(solution)/shard_map/reduce_scatter | solution.py:245
  600.3 30.8 %reduce-scatter.13.cloned.1.call-done = bf16[1,256,1024]{2,1,0:T(8,128)(2,1)} async-done(((bf16[1,2048,1024]{2,1,0:T(8,128)(2,1)}), bf16[1,256,1024]{2,1,0:T(8,128)(2,1)}) %reduce-scatter.13.cloned.1.call-update) | async-done | bytes 524304 | tf_op jit(solution)/shard_map/reduce_scatter | solution.py:248
  631.1 15.2 fusion.48
  646.4 11.5 fusion.47
  662.8 5.2 reduce-scatter.15.cloned.1.call-done
  672.3 21.9 %reduce-scatter.9.cloned.1.call-done = bf16[1,128,2048]{2,1,0:T(8,128)(2,1)} async-done(((bf16[1,256,2048]{2,1,0:T(8,128)(2,1)}), bf16[1,128,2048]{2,1,0:T(8,128)(2,1)}) %reduce-scatter.9.cloned.1.call-update) | async-done | bytes 524304 | tf_op jit(solution)/shard_map/reduce_scatter | solution.py:274
  694.1 3.8 convert_reduce_fusion.3
  698.0 18.0 %convolution_bitcast_fusion.1 = f32[2048,5120]{0,1:T(8,128)} fusion(bf16[1,256,4096]{2,1,0:T(8,128)(2,1)} %get-tuple-element.502, bf16[1,256,1024]{2,1,0:T(8,128)(2,1)S(1)} %copy-done.5, bf16[1,256,2048]{2,1,0:T(8,128)(2,1)} %all-gather.16.cloned.1.call-done), kind=kOutput, calls=%fused_computation.58 | convolution fusion | flops 5373952000 | bytes 45613056 | tf_op jit(solution)/shard_map/rtn,rtc->nc/dot_general | solution.py:195
  716.0 38.8 %copy.148 = f32[2048,5120]{1,0:T(8,128)} copy(f32[2048,5120]{0,1:T(8,128)} %convolution_bitcast_fusion.1) | data formatting | bytes 83886080
  756.0 23.1 %fusion.65 = f32[2048,7168]{1,0:T(8,128)} fusion(bf16[1,256,2048]{2,1,0:T(8,128)(2,1)} %all-gather.8.cloned.1.call-done, bf16[1,256,4096]{2,1,0:T(8,128)(2,1)S(1)} %get-tuple-element.501, bf16[1,256,1024]{2,1,0:T(8,128)(2,1)} %reduce-scatter.13.cloned.1.call-done, bf16[1,256,1024]{2,1,0:T(8,128)(2,1)S(1)} %copy-done.6, bf16[1,256,1024]{2,1,0:T(8,128)(2,1)S(1)} %copy-done.7), kind=kOutput, calls=%fused_computation.114 | convolution fusion | flops 7530872832 | bytes 63438848 | tf_op jit(solution)/shard_map/rtn,rtc->nc/dot_general | solution.py:268
  779.1 60.3 %all-reduce.3.cloned.1.call-done = (f32[2048]{0:T(1024)}, f32[2048]{0:T(1024)}, f32[2,7168]{1,0:T(2,128)}, f32[2048]{0:T(1024)}) async-done(((f32[2048]{0:T(1024)}, f32[2048]{0:T(1024)}, f32[2,7168]{1,0:T(2,128)}, f32[2048]{0:T(1024)}), (f32[2048]{0:T(1024)}, f32[2048]{0:T(1024)}, f32[2,7168]{1,0:T(2,128)}, f32[2048]{0:T(1024)})) %all-reduce.3.cloned.1.call-update) | async-done | bytes 81936 | tf_op jit(solution)/shard_map/psum | solution.py:291
  841.6 353.5 %reduce-scatter.19.cloned.1.call-done = f32[32,5120]{1,0:T(8,128)} async-done(((f32[2048,5120]{1,0:T(8,128)}), f32[32,5120]{1,0:T(8,128)}) %reduce-scatter.19.cloned.1.call-update) | async-done | bytes 655376
  1198.6 388.2 %reduce-scatter.17.cloned.1.call-done = f32[32,7168]{1,0:T(8,128)} async-done(((f32[2048,7168]{1,0:T(8,128)}), f32[32,7168]{1,0:T(8,128)}) %reduce-scatter.17.cloned.1.call-update) | async-done | bytes 917520 | tf_op jit(solution)/shard_map/reduce_scatter | solution.py:267
  (262 shorter events, 149.1 us)
Async XLA Ops:
  7.2 10.5 copy-start.10
  7.2 10.5 copy-start.16
  7.2 11.3 copy-start.21
  7.2 32.9 %all-gather.8.cloned.1.call-start = ((), (), s32[]{:S(2)}) async-start(), calls=%async_computation.6 | async-start | bytes 1572864 | tf_op jit(solution)/shard_map/all_gather | solution.py:100
  8.5 3.3 copy-start.19
  14.1 194.7 %all-gather.10.cloned.1.call-start = ((), (), s32[]{:S(2)}) async-start(), calls=%async_computation.7 | async-start | bytes 29818880 | tf_op jit(solution)/shard_map/all_gather | solution.py:109
  16.8 222.1 %all-gather.16.cloned.1.call-start = ((), (), s32[]{:S(2)}) async-start(), calls=%async_computation.11 | async-start | bytes 1572864 | tf_op jit(solution)/shard_map/all_gather | solution.py:101
  17.6 350.2 %all-gather.14.cloned.1.call-start = ((), (), s32[]{:S(2)}) async-start(), calls=%async_computation.9 | async-start | bytes 21299200 | tf_op jit(solution)/shard_map/all_gather | solution.py:180
  18.4 387.3 %all-gather.18.cloned.1.call-start = ((), (), s32[]{:S(2)}) async-start(), calls=%async_computation.16 | async-start | bytes 4718592 | tf_op jit(solution)/shard_map/all_gather | solution.py:125
  222.4 2.9 copy-start.2
  229.6 3.1 copy-start.13
  232.7 212.3 %all-gather.12.cloned.1.call-start = ((), (), s32[]{:S(2)}) async-start(), calls=%async_computation.8 | async-start | bytes 4718592 | tf_op jit(solution)/shard_map/all_gather | solution.py:124
  235.5 132.3 %copy-start.14 = (f32[256,16]{0,1:T(8,128)}, f32[256,16]{0,1:T(8,128)S(1)}, u32[]{:S(2)}) copy-start(f32[256,16]{0,1:T(8,128)S(1)} %get-tuple-element.524) | copy-start | bytes 49156
  238.3 353.4 %reduce-scatter.11.cloned.1.call-start = ((), (), s32[]{:S(2)}) async-start(), calls=%async_computation.12 | async-start | bytes 4718592 | tf_op jit(solution)/shard_map/reduce_scatter | solution.py:245
  451.3 6.3 copy-start.9
  451.3 6.3 copy-start.17
  552.5 78.6 %reduce-scatter.13.cloned.1.call-start = ((), (), s32[]{:S(2)}) async-start(), calls=%async_computation.13 | async-start | bytes 4718592 | tf_op jit(solution)/shard_map/reduce_scatter | solution.py:248
  559.0 109.0 %reduce-scatter.15.cloned.1.call-start = ((), (), s32[]{:S(2)}) async-start(), calls=%async_computation.14 | async-start | bytes 1572864 | tf_op jit(solution)/shard_map/reduce_scatter | solution.py:277
  560.7 7.7 copy-start.8
  568.4 26.9 %copy-start.15 = (f32[256,16]{0,1:T(8,128)S(1)}, f32[256,16]{0,1:T(8,128)}, u32[]{:S(2)}) copy-start(f32[256,16]{0,1:T(8,128)} %copy-done.14) | copy-start | bytes 49156
  646.3 47.8 %reduce-scatter.9.cloned.1.call-start = ((), (), s32[]{:S(2)}) async-start(), calls=%async_computation.10 | async-start | bytes 1572864 | tf_op jit(solution)/shard_map/reduce_scatter | solution.py:274
  657.9 181.5 %all-reduce.3.cloned.1.call-start = ((), (), s32[]{:S(2)}) async-start(), calls=%async_computation.18 | async-start | bytes 163840 | tf_op jit(solution)/shard_map/psum | solution.py:291
  659.0 3.1 copy-start.26
  659.0 9.0 copy-start
  659.0 9.0 copy-start.12
  659.0 9.0 copy-start.20
  660.0 10.1 copy-start.28
  660.0 10.1 copy-start.24
  660.0 34.2 %copy-start.18 = (f32[2048]{0:T(1024)S(1)}, f32[2048]{0:T(1024)}, u32[]{:S(2)}) copy-start(f32[2048]{0:T(1024)} %convert_element_type.205) | copy-start | bytes 24580
  661.5 36.5 %copy-start.5 = (bf16[1,256,1024]{2,1,0:T(8,128)(2,1)S(1)}, bf16[1,256,1024]{2,1,0:T(8,128)(2,1)}, u32[]{:S(2)}) copy-start(bf16[1,256,1024]{2,1,0:T(8,128)(2,1)} %copy.128) | copy-start | bytes 1572868
  698.0 497.2 %reduce-scatter.19.cloned.1.call-start = ((), (), s32[]{:S(2)}) async-start(), calls=%async_computation.17 | async-start | bytes 42598400
  754.9 831.9 %reduce-scatter.17.cloned.1.call-start = ((), (), s32[]{:S(2)}) async-start(), calls=%async_computation.15 | async-start | bytes 59637760 | tf_op jit(solution)/shard_map/reduce_scatter | solution.py:267
  (10 other events, 11.8 us)
Sparse Core Ops, SparseCore 0:
  14.2 25.8 all-gather.7
  42.4 166.3 all-gather.9
  210.5 24.6 all-gather.15
  237.3 130.4 all-gather.13
  369.9 35.7 all-gather.17
  407.8 37.0 all-gather.11
  552.7 38.9 reduce-scatter.10
  594.1 36.9 reduce-scatter.12
  646.4 21.5 reduce-scatter.14
  670.3 23.7 reduce-scatter.8
  700.7 138.6 all-reduce.2
  841.8 353.2 reduce-scatter.18
  1197.7 388.9 reduce-scatter.16
where the time goes:
time: 1610 us; the launch traced here: 1600 us
  waiting for transfers between devices  1250 us (78%)
  matrix products  147 us (9%)
  local copies, waits for them, and re-layouts  137 us (9%)
  other arithmetic  47.9 us (3%)
    reduce_scatter x1, waiting for transfers between devices, shards(): lax.psum_scatter(jnp.einsum('rtn,rtc->nc', columns, grad_entry, preferred...  388 us
    unnamed x14, waiting for transfers between devices  354 us
    all_gather x1, waiting for transfers between devices, shards(): lax.all_gather(weights_in, ('dp', 'seq'), axis=0, tiled=True)  169 us
    all_gather x1, waiting for transfers between devices, shards(): lax.all_gather(weights_out, ('dp', 'seq'), axis=0, tiled=True)  129 us
    unnamed x64, local copies, waits for them, and re-layouts  65.5 us
    psum x1, waiting for transfers between devices, shards(): lax.psum((slot_terms, grad_gain, grad_shift, out_bias_terms), ('dp', 'seq...  60.3 us
  transfers between devices with their start and end apart: 13, of which 12 were waited for; matrix products, arithmetic and copies ran while one was open for 11% of the time, Pallas kernels for 0%

commit v1 on v0

v1 whole, which is shorter than its diff:
```python
import functools

import jax
import jax.numpy as jnp
import numpy as np
from jax import lax
from jax.experimental import pallas as pl
from jax.experimental.pallas import tpu as pltpu
from jax.sharding import PartitionSpec as P


HD = 64
ROT = 32
EPSILON = 1e-05
MASKED = -1e30
MESH = pl.DeviceIdType.MESH
BF = jnp.bfloat16
F32 = jnp.float32

D = 2048
T = 2048
CQ = 128
CF = 512
CI = 3 * CQ + CF
CO = CQ + CF
CS = CI + 256
BLK = 256
NB = T // BLK
QB = 512
NQ = T // QB
VMEM_LIMIT = 65400 * 1024
SLOTS = 224


def dot(a, b):
    return lax.dot_general(a, b, (((1,), (0,)), ((), ())), preferred_element_type=F32)


def dot_nt(a, b):
    return lax.dot_general(a, b, (((1,), (1,)), ((), ())), preferred_element_type=F32)


def loop(n, body, events=()):
    def run(i, carry):
        body(i)
        for when, event in events:
            pl.when(i == when)(event)
        return carry

    lax.fori_loop(0, n, run, 0)


def pieces(n, step, body):
    loop(n // step, lambda i: body(pl.multiple_of(i * step, step)))


class Net:
    def __init__(self, send_sems, recv_sems, credits):
        self.credits = credits
        self.dp, self.seq, self.branch = (lax.axis_index(n) for n in ("dp", "seq", "branch"))
        self.x, self.yl = lax.rem(self.dp, 4), lax.div(self.dp, 4)
        self.z, self.core = lax.div(self.seq, 2), lax.rem(self.seq, 2)
        self.send_sems, self.recv_sems = send_sems, recv_sems
        self.slots, self.sent = {}, []
        self.right, self.left = self.at(dz=1), self.at(dz=3)
        self.sib, self.mate = self.at(dc=1), self.at(db=1)
        self.xright, self.xleft, self.ymate = self.at(dx=1), self.at(dx=3), self.at(dy=1)

    def at(self, dx=0, dy=0, dz=0, dc=0, db=0):
        x, yl = lax.rem(self.x + dx, 4), lax.rem(self.yl + dy, 2)
        z, core = lax.rem(self.z + dz, 4), lax.rem(self.core + dc, 2)
        return (yl * 4 + x, z * 2 + core, lax.rem(self.branch + db, 2))

    def seq_peer(self, d):
        return (self.dp, lax.rem(self.seq + d, 8), self.branch)

    def dp_peer(self, d):
        return (lax.rem(self.dp + d, 8), self.seq, self.branch)

    def greet(self, devices):
        barrier = pltpu.get_barrier_semaphore()
        for device in devices:
            pl.semaphore_signal(barrier, inc=1, device_id=device, device_id_type=MESH)
        return lambda: pl.semaphore_wait(barrier, len(devices))

    def slot(self, key):
        return self.slots.setdefault(key, len(self.slots))

    def copy(self, key, src, dst, to):
        index = self.slot(key)
        return pltpu.make_async_remote_copy(
            src_ref=src,
            dst_ref=dst,
            send_sem=self.send_sems.at[index],
            recv_sem=self.recv_sems.at[index],
            device_id=to,
            device_id_type=MESH,
        )

    def send(self, key, src, dst, to, like=None):
        self.copy(key, src, dst, to).start()
        self.sent.append((key, src if like is None else like))

    def recv(self, key, dst):
        self.copy(key, dst, dst, self.sib).wait_recv()

    def drain(self, tag=None):
        for key, like in self.sent:
            if tag is None or key[0] == tag:
                self.copy(key, like, like, self.sib).wait_send()
        self.sent = [(key, like) for key, like in self.sent if tag is not None and key[0] != tag]

    def allow(self, index, devices):
        for device in devices:
            pl.semaphore_signal(self.credits.at[index], inc=1, device_id=device, device_id_type=MESH)


class Local:
    def __init__(self, sems):
        self.sems, self.count, self.open = sems, 0, []

    def start(self, src, dst, keep=True):
        copy = pltpu.make_async_copy(src, dst, self.sems.at[self.count])
        self.count += 1
        copy.start()
        if keep:
            self.open.append(copy)
        return copy

    def finish(self):
        for copy in self.open:
            copy.wait()
        self.open = []


class Gather:
    def __init__(self, net, tag, buf, rows, n, ring, right, left, mate, sib=None, across=None):
        self.net, self.tag, self.buf, self.n = net, tag, buf, n
        self.right, self.left, self.mate, self.sib, self.across = right, left, mate, sib, across
        self.starts = {
            (dr, rel, other): rows(lax.rem(ring + dr, 4), rel, other)
            for dr in range(4)
            for rel in (0, 1)
            for other in ((False, True) if sib is not None else (False,))
        }

    def view(self, dr, rel, lo=0, n=None, other=False):
        start = self.starts[dr, rel, other] + lo
        return self.buf.at[pl.ds(pl.multiple_of(start, 16), self.n if n is None else n)]

    def _send(self, key, view, to):
        self.net.send((self.tag,) + key, view, view, to, self.buf.at[pl.ds(0, view.shape[0])])

    def _recv(self, key, view):
        self.net.recv((self.tag,) + key, view)

    def to_sib(self, dr, rel):
        if self.sib is not None:
            self._send(("s", dr, rel), self.view(dr, rel), self.sib)

    def start_mate(self):
        self._send(("m",), self.view(0, 0), self.mate)

    def start_ring(self, rel=0):
        view = self.view(0, rel)
        self._send(("r", rel), view, self.right)
        self._send(("l", rel), view, self.left)
        if self.across is not None:
            self._send(("a", rel), view, self.across)
        self.to_sib(0, rel)

    def from_mate(self):
        self._recv(("m",), self.view(0, 1))
        self.start_ring(1)

    def direct(self):
        for rel in (0, 1):
            for key, dr in (("r", 3), ("l", 1), ("a", 2)):
                self._recv((key, rel), self.view(dr, rel))

    def near(self, rel):
        half = self.n // 2
        self._recv(("r", rel), self.view(3, rel))
        self._send(("rr", rel), self.view(3, rel, 0, half), self.right)
        self.to_sib(3, rel)
        self._recv(("l", rel), self.view(1, rel))
        self._send(("ll", rel), self.view(1, rel, half, half), self.left)
        self.to_sib(1, rel)

    def far(self, rel):
        half = self.n // 2
        self._recv(("rr", rel), self.view(2, rel, 0, half))
        self._recv(("ll", rel), self.view(2, rel, half, half))
        self.to_sib(2, rel)

    def from_sib(self, dr):
        for rel in (0, 1):
            self._recv(("s", dr, rel), self.view(dr, rel, other=True))


def token_rows(net):
    def rows(ring, rel, other):
        core = lax.rem(net.core + (1 if other else 0), 2)
        return (ring * 2 + core) * 256 + lax.rem(net.branch + rel, 2) * 128

    return rows


def weight_rows(net):
    def rows(ring, rel, other):
        return (lax.rem(net.yl + rel, 2) * 4 + ring) * 256

    return rows


def norm_stats(x):
    mean = jnp.mean(x, -1, keepdims=True)
    centred = x - mean
    variance = jnp.mean(centred * centred, -1, keepdims=True)
    rstd = lax.rsqrt(variance + EPSILON)
    return centred * rstd, rstd


def roll_lanes(x, shift):
    return pltpu.roll(x, shift % x.shape[1], 1)


def rotate(x, cos, sine):
    lane = lax.broadcasted_iota(jnp.int32, x.shape, 1) & (HD - 1)
    return x * cos + jnp.where(lane < ROT // 2, roll_lanes(x, -16), roll_lanes(x, 16)) * sine


def scores_of(keys, queries, key_ids, seg_row, behind=None):
    s = dot_nt(keys, queries)
    allowed = jnp.concatenate([key_ids] * (2 * QB // 128), 1) == seg_row
    if behind is not None:
        key_at = lax.broadcasted_iota(jnp.int32, s.shape, 0) + behind
        query_at = lax.broadcasted_iota(jnp.int32, s.shape, 1) & (QB - 1)
        allowed = (allowed & (key_at <= query_at)) | (key_at == query_at)
    return jnp.where(allowed, s, MASKED)


class Scatter:
    def __init__(self, net, tag, view, near, far, mate_buf, n, right, left, mate):
        self.net, self.tag, self.view, self.near, self.far, self.mate_buf = net, tag, view, near, far, mate_buf
        self.right, self.left, self.mate, self.n, self.half = right, left, mate, n, n // 2
        self.like, self.whole = far(0, 0), mate_buf

    def _send(self, key, src, dst, to):
        self.net.send((self.tag,) + key, src, dst, to, self.like)

    def _recv(self, key):
        self.net.recv((self.tag,) + key, self.like)

    def begin(self, rel):
        half = self.half
        self._send(("rr", rel), self.view(2, rel, 0, half), self.far(0, rel), self.right)
        self._send(("ll", rel), self.view(2, rel, half, half), self.far(1, rel), self.left)

    def begin_near(self, rel):
        half = self.half
        self._send(("rb", rel), self.view(1, rel, half, half), self.near(0, rel).at[pl.ds(half, half)], self.right)
        self._send(("lt", rel), self.view(3, rel, 0, half), self.near(1, rel).at[pl.ds(0, half)], self.left)

    def middle(self, rel):
        for key, dr, way, lo, done, to in (
            ("rr", 1, 0, 0, "rt", self.right),
            ("ll", 3, 1, self.half, "lb", self.left),
        ):
            self._recv((key, rel))

            step = 32 if self.half % 32 == 0 else 16

            def add(first):
                part = self.view(dr, rel, lo + first, step)
                part[...] = (part[...].astype(F32) + self.far(way, rel)[pl.ds(first, step), :].astype(F32)).astype(BF)

            pieces(self.half, step, add)
            view = self.view(dr, rel, lo, self.half)
            self._send((done, rel), view, self.near(way, rel).at[pl.ds(lo, self.half)], to)

    def end(self, rel):
        for key in ("rb", "rt", "lt", "lb"):
            self._recv((key, rel))

        def add(first):
            view, at = self.view(0, rel, first, 32), pl.ds(first, 32)
            total = view[...].astype(F32) + self.near(0, rel)[at, :].astype(F32) + self.near(1, rel)[at, :].astype(F32)
            view[...] = total.astype(BF)

        pieces(self.n, 32, add)

    def to_mate(self):
        self.net.send(("m" + self.tag,), self.view(0, 1, 0, self.n), self.whole, self.mate, self.whole)

    def last(self):
        self.net.recv(("m" + self.tag,), self.whole)

    def total(self, first, n):
        return self.view(0, 0, first, n)[...].astype(F32) + self.mate_buf[pl.ds(first, n), :].astype(F32)


class AllSum:
    def __init__(self, net, tag, vec, seq_buf, dp_buf, mate_buf):
        self.net, self.tag, self.vec = net, tag, vec
        self.seq_buf, self.dp_buf, self.mate_buf = seq_buf, dp_buf, mate_buf

    def _spread(self, key, buf, me, peer):
        buf[me] = self.vec[...]
        for d in range(1, 8):
            self.net.send((self.tag, key, d), buf.at[me], buf.at[me], peer(d))

    def _total(self, key, buf, me):
        for d in range(1, 8):
            self.net.recv((self.tag, key, d), buf.at[lax.rem(me + 8 - d, 8)])
        total = buf[0]
        for s in range(1, 8):
            total = total + buf[s]
        self.vec[...] = total

    def start(self):
        self._spread("d", self.dp_buf, self.net.dp, self.net.dp_peer)

    def second(self):
        self._total("d", self.dp_buf, self.net.dp)
        self.net.send((self.tag, "b"), self.vec, self.mate_buf, self.net.mate)

    def third(self):
        self.net.recv((self.tag, "b"), self.mate_buf)
        self.seq_buf[self.net.seq] = self.vec[...] + self.mate_buf[...]
        mine = self.seq_buf.at[self.net.seq]
        for d in range(1, 8):
            self.net.send((self.tag, "q", d), mine, mine, self.net.seq_peer(d))

    def done(self):
        me = self.net.seq
        for d in range(1, 8):
            self.net.recv((self.tag, "q", d), self.seq_buf.at[lax.rem(me + 8 - d, 8)])
        total = self.seq_buf[0]
        for s in range(1, 8):
            total = total + self.seq_buf[s]
        return total


class PairFirst(Scatter):
    def give(self, dr):
        for src, dst in zip(self._cuts(dr), self.mate_buf(dr)):
            self.net.send(("p" + self.tag, dr, src[1]), src[0], dst, self.mate)

    def _cuts(self, dr):
        refs = self.mate_buf(dr)
        n = self.n // len(refs)
        return [(self.view(dr, 1, i * n, n), i) for i in range(len(refs))]

    def take(self, dr):
        for i, ref in enumerate(self.mate_buf(dr)):
            self.net.recv(("p" + self.tag, dr, i), ref)
            n = self.n // len(self.mate_buf(dr))

            def add(first, i=i, n=n, ref=ref):
                mine = self.view(dr, 0, i * n + first, 16)
                mine[...] = (mine[...].astype(F32) + ref[pl.ds(first, 16), :].astype(F32)).astype(BF)

            pieces(n, 16, add)

    def total(self, first, n):
        return self.view(0, 0, first, n)[...].astype(F32)


def turn_weights(scatter, send_buf):
    def turn(first):
        send_buf[:, pl.ds(first, 128)] = scatter.total(first, 128).T.astype(BF)

    pieces(scatter.n, 128, turn)


def send_weights(net, tag, width, send_buf, recv_buf):
    columns = pl.ds(0, width)
    for d in range(1, 8):
        to = lax.rem(net.seq + d, 8)
        src = send_buf.at[pl.ds(pl.multiple_of(to * 32, 32), 32), columns]
        net.send((tag, d), src, recv_buf.at[net.seq], net.seq_peer(d))
    recv_buf[net.seq] = send_buf[pl.ds(pl.multiple_of(net.seq * 32, 32), 32), columns]


def receive_weights(net, tag, recv_buf):
    for d in range(1, 8):
        net.recv((tag, d), recv_buf.at[lax.rem(net.seq + 8 - d, 8)])


def ring_step(t):
    return jnp.where(t == 0, 2, jnp.where(t == 1, 1, jnp.where(t == 2, 3, 0)))


def block_kernel(
    x_in, go_in, qkv_in, up_in, att_in, down_in, seg_in, valid_in, vectors_in, qkv_b, rates_in,
    n_out, output_ref, ginp_ref, sums_ref, bias_ref, wo_ref, wu_ref, wq_ref,
    n_buf, g_buf, sib_buf, wq, wu, wo, tab, kid, segs, qst, k, v, kt, vt, mix, mixt, dgel, ot,
    dost, dk, dv, lse, delta, m_ref, l_ref, acc_ref, bias,
    near, far, mate_buf, gw, wnear, wfar, wmate, wsend, wrecv_o, wrecv_u, wrecv_q,
    bsum, bdp, bseq, vec, vseq, vdp, vmate,
    send_sems, recv_sems, local_sems, credits,
):
    net, local = Net(send_sems, recv_sems, credits), Local(local_sems)
    gain_in, shift_in, ob_in, up_b = (
        vectors_in.at[:, pl.ds(first, width)] for first, width in ((0, D), (D, D), (2 * D, D), (3 * D, 4096))
    )
    rows = token_rows(net)
    own = pl.ds(pl.multiple_of(rows(net.z, 0, False), 128), 128)
    get_x = local.start(x_in, vt, False)
    get_g = local.start(go_in, g_buf.at[own], False)
    dp_peers = [net.dp_peer(d) for d in range(1, 8)]
    all_here = net.greet([net.seq_peer(d) for d in range(1, 8)] + dp_peers + [net.mate])

    groups = (
        ("q", wq, [(qkv_in.at[j], CQ, j * CQ) for j in range(3)]),
        ("u", wu, [(up_in, CF, 0)]),
        ("o", wo, [(att_in, CQ, 0), (down_in, CF, CQ)]),
    )
    mine = pl.ds(pl.multiple_of(net.dp * 256 + net.seq * 32, 32), 32)

    def cuts(to, group):
        name, buf, parts = group
        return [
            (src.at[:, pl.ds(pl.multiple_of(to * width, 128), width)], buf.at[mine, pl.ds(first, width)])
            for src, width, first in parts
        ]

    own_parts = [local.start(src, dst, False) for group in groups for src, dst in cuts(net.seq, group)]

    def send_pieces(group):
        for d in range(1, 8):
            for src, dst in cuts(lax.rem(net.seq + d, 8), group):
                net.copy(("p" + group[0], d), src, dst, net.seq_peer(d)).start()
            net.sent.append((("p" + group[0], d), group[1].at[mine]))

    def receive_pieces(group):
        for d in range(1, 8):
            sender = net.dp * 256 + lax.rem(net.seq + 8 - d, 8) * 32
            net.recv(("p" + group[0], d), group[1].at[pl.ds(pl.multiple_of(sender, 32), 32)])

    get_x.wait()

    def norm(first):
        xhat, unused = norm_stats(vt[pl.ds(first, 32), :].astype(F32))
        at = pl.ds(pl.multiple_of(rows(net.z, 0, False) + first, 32), 32)
        n_buf[at, :] = (xhat * gain_in[...].astype(F32) + shift_in[...].astype(F32)).astype(BF)

    pieces(128, 32, norm)
    ag_n = Gather(net, "n", n_buf, rows, 128, net.z, net.right, net.left, net.mate, net.sib)
    ag_g = Gather(net, "g", g_buf, rows, 128, net.z, net.right, net.left, net.mate, net.sib)
    wrows = weight_rows(net)
    ag_q, ag_u, ag_o = (
        Gather(net, name, buf, wrows, 256, net.x, net.xright, net.xleft, net.ymate) for name, buf, parts in groups
    )
    all_here()
    send_pieces(groups[0])
    ag_n.start_mate()
    ag_n.start_ring()
    for copy in own_parts:
        copy.wait()
    receive_pieces(groups[0])
    ag_q.start_mate()
    ag_q.start_ring()

    for j in range(3):
        bias[:, j * CQ : (j + 1) * CQ] = qkv_b[j : j + 1, pl.ds(pl.multiple_of(net.seq * CQ, CQ), CQ)].astype(F32)
    bias[:, 3 * CQ :] = up_b[:, pl.ds(pl.multiple_of(net.seq * CF, CF), CF)].astype(F32)
    seg = seg_in[...].astype(F32)
    valid = valid_in[...].astype(F32)
    starts = [jnp.sum((seg < d).astype(F32), 1, keepdims=True) for d in range(1, 5)]
    for i in range(NQ):
        part_seg = seg[:, i * QB : (i + 1) * QB]
        segs[i] = jnp.concatenate([part_seg, part_seg], 1)
    key_seg = jnp.where(valid == 1.0, seg, -1.0)
    for i in range(T // 128):
        at = slice(i * 128, (i + 1) * 128)
        kid[at, :] = jnp.broadcast_to(key_seg[:, at], (128, 128)).T
        seg_col = jnp.broadcast_to(seg[:, at], (128, 128)).T
        first = jnp.zeros((128, 128), F32)
        for d in range(1, 5):
            first = jnp.where(seg_col >= d, jnp.broadcast_to(starts[d - 1], (128, 128)), first)
        index = (lax.broadcasted_iota(jnp.int32, (128, 128), 0) + i * 128).astype(F32)
        tab[0, at, :] = index - first

    def table(i):
        at = pl.ds(pl.multiple_of(i * BLK, BLK), BLK)
        angle = tab[0, at, :] * rates_in[...]
        lane = lax.broadcasted_iota(jnp.int32, (BLK, 128), 1) & (HD - 1)
        sine = jnp.sin(angle)
        tab[0, at, :] = jnp.where(lane < ROT, jnp.cos(angle), 1.0)
        tab[1, at, :] = jnp.where(lane < ROT // 2, -sine, jnp.where(lane < ROT, sine, 0.0))

    loop(NB, table)

    def entry(i):
        at = pl.ds(pl.multiple_of(i * BLK, BLK), BLK)
        t = dot(n_buf[at, :], wq[...]) + bias[:, : 3 * CQ]
        cos, sine = tab[0, at, :], tab[1, at, :]
        lane = lax.broadcasted_iota(jnp.int32, (BLK, CQ), 1)
        q = rotate(t[:, :CQ], cos, sine).astype(BF).astype(F32) * HD ** (-0.5)
        block, first = lax.div(i, 2), pl.multiple_of(lax.rem(i, 2) * BLK, BLK)
        qst[block, pl.ds(first, BLK), :] = jnp.where(lane < HD, q, 0.0).astype(BF)
        qst[block, pl.ds(first + QB, BLK), :] = jnp.where(lane < HD, 0.0, q).astype(BF)
        key = rotate(t[:, CQ : 2 * CQ], cos, sine)
        k[at, :] = key.astype(BF)
        kt[:, at] = key.T.astype(BF)
        value = t[:, 2 * CQ :]
        v[at, :] = value.astype(BF)
        vt[:, at] = value.T.astype(BF)

    def up_entry(i):
        at = pl.ds(pl.multiple_of(i * BLK, BLK), BLK)
        h = dot(n_buf[at, :], wu[...]) + bias[:, 3 * CQ :]
        square = h * h
        th = jnp.tanh(0.7978845608028654 * h * (1.0 + 0.044715 * square))
        act = 0.5 * h * (1.0 + th)
        slope = 0.5 * (1.0 + th) + 0.5 * h * (1.0 - th * th) * (
            0.7978845608028654 * (1.0 + 3 * 0.044715 * square)
        )
        mix[at, CQ:CO] = act.astype(BF)
        mixt[CQ:CO, at] = act.T.astype(BF)
        for part in (0, 1):
            dgel[lax.div(i, 2), lax.rem(i, 2), part * BLK : (part + 1) * BLK, :] = slope[
                :, part * BLK : (part + 1) * BLK
            ].astype(BF)

    def on_place(dr, work):
        first = lax.rem(net.z + dr, 4) * 2
        loop(2, lambda t: work(first + t))

    get_g.wait()
    ag_q.from_mate()
    ag_n.from_mate()
    send_pieces(groups[1])
    send_pieces(groups[2])
    ag_q.near(0)
    ag_n.near(0)
    ag_q.near(1)
    ag_g.start_mate()
    ag_q.far(0)
    ag_q.far(1)
    ag_n.from_sib(0)
    on_place(0, entry)
    receive_pieces(groups[1])
    ag_u.start_mate()
    ag_u.start_ring()
    ag_n.near(1)
    ag_n.from_sib(3)
    on_place(3, entry)
    ag_n.from_sib(1)
    on_place(1, entry)
    ag_u.from_mate()
    receive_pieces(groups[2])
    ag_o.start_mate()
    ag_o.start_ring()
    ag_n.far(0)
    ag_u.near(0)
    ag_n.far(1)
    ag_g.start_ring()
    ag_g.from_mate()
    ag_n.from_sib(2)
    on_place(2, entry)
    park = local.start(n_buf, n_out, False)

    def attend(i):
        at = pl.ds(pl.multiple_of(i * QB, QB), QB)
        queries, seg_row = qst[i], segs[i]

        def keys_at(j):
            return pl.ds(pl.multiple_of(j * BLK, BLK), BLK)

        def step(j, behind=None):
            kat = keys_at(j)
            s = scores_of(k[kat, :], queries, kid[kat, :], seg_row, behind)
            old = m_ref[...]
            top = jnp.maximum(old, jnp.max(s, 0, keepdims=True))
            fade = jnp.exp(old - top)
            p = jnp.exp(s - top)
            m_ref[...] = top
            l_ref[...] = l_ref[...] * fade + jnp.sum(p, 0, keepdims=True)
            acc_ref[...] = acc_ref[...] * fade + dot(vt[:, kat], p.astype(BF))

        kat = keys_at(2 * i)
        s = scores_of(k[kat, :], queries, kid[kat, :], seg_row, 0)
        top = jnp.max(s, 0, keepdims=True)
        p = jnp.exp(s - top)
        m_ref[...] = top
        l_ref[...] = jnp.sum(p, 0, keepdims=True)
        acc_ref[...] = dot(vt[:, kat], p.astype(BF))
        step(2 * i + 1, BLK)
        loop(2 * i, step)
        lse[i] = m_ref[...] + jnp.log(l_ref[...])
        both = acc_ref[...] / l_ref[...]
        heads = jnp.concatenate([both[:HD, :QB], both[HD:, QB:]], 0)
        ot[:, at] = heads
        mixt[:CQ, at] = heads.astype(BF)
        mix[at, :CQ] = heads.T.astype(BF)

    loop(NQ, attend, ((0, lambda: ag_u.near(1)), (0, ag_o.from_mate), (2, lambda: ag_u.far(0)), (2, lambda: ag_u.far(1))))
    ag_o.near(0)
    get_x = local.start(x_in, vt, False)
    loop(NB, up_entry, ((0, lambda: ag_o.near(1)), (2, lambda: ag_g.near(0)), (3, lambda: ag_g.near(1))))
    ag_o.far(0)
    ag_o.far(1)

    park.wait()
    net.drain("n")

    def chunk_view(buf):
        starts = {(dr, rel): rows(lax.rem(net.z + dr, 4), rel, False) for dr in range(4) for rel in (0, 1)}

        def view(dr, rel, lo, n):
            return buf.at[pl.ds(pl.multiple_of(starts[dr, rel] + lo, 16), n)]

        return view

    def block_rows(dr, other):
        core = lax.rem(net.core + (1 if other else 0), 2)
        return pl.ds(pl.multiple_of((lax.rem(net.z + dr, 4) * 2 + core) * 256, 256), 256)

    def partial_blocks(tag, buf, product, hooks):
        def other(dr):
            at = block_rows(dr, True)
            buf[at, :] = product(at).astype(BF)
            net.send((tag, dr), buf.at[at], sib_buf.at[dr], net.sib)

        def own(dr):
            at = block_rows(dr, False)
            value = product(at)
            net.recv((tag, dr), sib_buf.at[dr])
            buf[at, :] = (value + sib_buf[dr].astype(F32)).astype(BF)

        other(2)
        other(1)
        own(2)
        hooks[0]()
        other(3)
        hooks[1]()
        own(1)
        other(0)
        own(3)
        hooks[2]()
        own(0)

    def near_at(way, rel):
        return near.at[way, rel]

    def far_at(way, rel):
        return far.at[way, rel]

    out_view = chunk_view(n_buf)
    rs_out = Scatter(net, "t1", out_view, near_at, far_at, mate_buf, 128, net.right, net.left, net.mate)

    def nothing():
        pass

    def gather_end():
        ag_g.far(0)
        ag_g.far(1)
        for rel in (1, 0):
            rs_out.begin(rel)
            rs_out.begin_near(rel)

    partial_blocks("s1", n_buf, lambda at: dot_nt(mix[at, :CO], wo[...]), (nothing, nothing, gather_end))
    net.allow(0, [net.sib])
    for dr in range(4):
        ag_g.from_sib(dr)

    bsum[...] = jnp.zeros_like(bsum)

    def sum_rows(i):
        at = pl.ds(pl.multiple_of(i * BLK, BLK), BLK)
        mine = g_buf[at, pl.ds(pl.multiple_of(net.seq * 256, 256), 256)]
        bsum[:, CI:] += jnp.sum(mine.astype(F32), 0, keepdims=True)

    loop(NB, sum_rows)

    def back(i):
        at = pl.ds(pl.multiple_of(i * BLK, BLK), BLK)
        t = dot(g_buf[at, :], wo[...])
        lane = lax.broadcasted_iota(jnp.int32, (BLK, CQ), 1)
        do = t[:, :CQ].astype(BF).astype(F32)
        block, first = lax.div(i, 2), pl.multiple_of(lax.rem(i, 2) * BLK, BLK)
        dost[block, pl.ds(first, BLK), :] = jnp.where(lane < HD, do, 0.0).astype(BF)
        dost[block, pl.ds(first + QB, BLK), :] = jnp.where(lane < HD, 0.0, do).astype(BF)
        terms = do.T * ot[:, at]
        delta[block, :, pl.ds(first, BLK)] = jnp.sum(terms[:HD], 0, keepdims=True)
        delta[block, :, pl.ds(first + QB, BLK)] = jnp.sum(terms[HD:], 0, keepdims=True)
        for part in (0, 1):
            slope = dgel[lax.div(i, 2), lax.rem(i, 2), part * BLK : (part + 1) * BLK, :].astype(F32)
            grad = t[:, CQ + part * BLK : CQ + (part + 1) * BLK] * slope
            mix[at, 3 * CQ + part * BLK : 3 * CQ + (part + 1) * BLK] = grad.astype(BF)

    loop(NB, back)
    net.drain("o")
    net.allow(5, [net.xleft, net.xright, net.ymate])

    def weight_scatter(tag, buf, near_of, far_of, last_buf, width):
        return Scatter(
            net, tag, lambda dr, rel, lo, n: buf.at[dr, rel, pl.ds(lo, n)], near_of, far_of, last_buf, width,
            net.xright, net.xleft, net.ymate,
        )

    def sized(buf, n):
        return lambda way, rel: buf.at[way, rel, pl.ds(0, n)]

    def weight_chunks(scatter, buf, first, features):
        width = scatter.n

        def body(t):
            dr, rel = ring_step(lax.div(t, 2)), 1 - lax.rem(t, 2)
            dp = lax.rem(net.yl + rel, 2) * 4 + lax.rem(net.x + dr, 4)
            columns = pl.ds(pl.multiple_of(dp * 256, 256), 256)
            buf[dr, rel, :width] = dot(mixt[first : first + width, :], features[:, columns]).astype(BF)

        loop(
            NB,
            body,
            (
                (0, lambda: scatter.begin(1)), (1, lambda: scatter.begin(0)), (4, lambda: scatter.begin_near(1)),
                (5, lambda: scatter.begin_near(0)),
            ),
        )

    rs_o = weight_scatter("w1", gw, sized(wnear, CO), sized(wfar, CO // 2), wmate, CO)
    weight_chunks(rs_o, gw, 0, g_buf)
    net.drain("g")
    reload = local.start(n_out, g_buf, False)

    def put(at, first, value):
        width = value.shape[1]
        rounded = value.astype(BF)
        mix[at, first : first + width] = rounded
        mixt[first : first + width, at] = value.T.astype(BF)
        return jnp.sum(rounded.astype(F32), 0, keepdims=True)


    def turn_hidden(i):
        at = pl.ds(pl.multiple_of(i * BLK, BLK), BLK)
        grad = mix[at, 3 * CQ :].astype(F32)
        mixt[3 * CQ :, at] = grad.T.astype(BF)
        bsum[:, 3 * CQ : CI] += jnp.sum(grad, 0, keepdims=True)

    loop(NB, turn_hidden)
    reload.wait()
    rs_u = weight_scatter(
        "w2",
        dgel,
        lambda way, rel: wo.at[pl.ds((2 * way + rel) * CF, CF), pl.ds(0, 256)],
        lambda way, rel: wo.at[pl.ds((2 * way + rel) * 256, 256), pl.ds(256, 256)],
        wo.at[pl.ds(2 * CF, CF), pl.ds(256, 256)],
        CF,
    )
    pl.semaphore_wait(credits.at[5], 3)
    weight_chunks(rs_u, dgel, 3 * CQ, g_buf)

    def block(i):
        at = pl.ds(pl.multiple_of(i * QB, QB), QB)
        queries, dos, seg_row, log_total, shift = qst[i], dost[i], segs[i], lse[i], delta[i]
        acc_ref[...] = jnp.zeros_like(acc_ref)

        def tile(j, behind=None):
            kat = pl.ds(pl.multiple_of(j * BLK, BLK), BLK)
            s = scores_of(k[kat, :], queries, kid[kat, :], seg_row, behind)
            p = jnp.exp(s - log_total)
            ds = (p * (dot_nt(v[kat, :], dos) - shift)).astype(BF)
            acc_ref[...] += dot(kt[:, kat], ds)
            return kat, dot(p.astype(BF), dos), dot(ds, queries)

        for c in (0, 1):
            kat, add_v, add_k = tile(2 * i + c, c * BLK)
            dv[kat, :] = add_v
            dk[kat, :] = add_k

        def step(j):
            kat, add_v, add_k = tile(j)
            dv[kat, :] += add_v
            dk[kat, :] += add_k

        loop(2 * i, step)
        dq = jnp.concatenate([acc_ref[:HD, :QB], acc_ref[HD:, QB:]], 0).T * HD ** (-0.5)
        bsum[:, :CQ] += put(at, 0, rotate(dq, tab[0, at, :], -tab[1, at, :]))

    loop(
        NQ,
        block,
        (
            (1, lambda: rs_out.middle(1)), (2, lambda: rs_out.middle(0)), (2, lambda: rs_o.middle(1)),
            (2, lambda: rs_o.middle(0)), (3, lambda: rs_out.end(1)), (3, rs_out.to_mate), (3, lambda: rs_o.end(1)),
            (3, rs_o.to_mate),
        ),
    )

    def finish_keys(i):
        at = pl.ds(pl.multiple_of(i * BLK, BLK), BLK)
        bsum[:, CQ : 2 * CQ] += put(at, CQ, rotate(dk[at, :], tab[0, at, :], -tab[1, at, :]))
        bsum[:, 2 * CQ : 3 * CQ] += put(at, 2 * CQ, dv[at, :])

    loop(NB, finish_keys)

    rs_o.end(0)
    net.allow(2, [net.xleft, net.xright])
    rs_out.end(0)
    net.allow(1, [net.left, net.right])
    net.allow(6, [net.mate])
    net.drain("s1")
    net.drain("t1")
    pl.semaphore_wait(credits.at[0], 1)
    pl.semaphore_wait(credits.at[1], 2)
    rs_in = Scatter(
        net,
        "t2",
        out_view,
        lambda way, rel: near.at[way, rel, pl.ds(0, 96)],
        lambda way, rel: far.at[way, rel, pl.ds(0, 48)],
        mate_buf.at[pl.ds(0, 96)],
        96,
        net.right,
        net.left,
        net.mate,
    )
    from_mate = {
        2: [near.at[0, 1, pl.ds(96, 32)]],
        1: [near.at[1, 1, pl.ds(96, 32)]],
        3: [far.at[0, 1, pl.ds(48, 16)], far.at[1, 1, pl.ds(48, 16)]],
        0: [mate_buf.at[pl.ds(96, 32)]],
    }
    rs_pair = PairFirst(
        net,
        "t3",
        lambda dr, rel, lo, n: out_view(dr, rel, lo + 96, n),
        lambda way, rel: near.at[way, rel, pl.ds(96, 32)],
        lambda way, rel: far.at[way, rel, pl.ds(48, 16)],
        from_mate.get,
        32,
        net.right,
        net.left,
        net.mate,
    )
    pl.semaphore_wait(credits.at[6], 1)

    def begin():
        rs_in.begin(1)
        rs_in.begin(0)
        rs_pair.give(2)

    def begin_up():
        rs_u.middle(1)
        rs_u.middle(0)

    def output_ends():
        rs_in.begin_near(1)
        rs_in.begin_near(0)
        rs_pair.give(1)
        rs_pair.give(3)
        rs_out.last()
        get_x.wait()

        def residual(first):
            at = pl.ds(first, 32)
            kt[at, :] = (vt[at, :].astype(F32) + rs_out.total(first, 32) + ob_in[...].astype(F32)).astype(BF)

        pieces(128, 32, residual)
        net.drain("mt1")
        net.allow(3, [net.mate])

    partial_blocks(
        "s2",
        n_buf,
        lambda at: dot_nt(mix[at, : 3 * CQ], wq[...]) + dot_nt(mix[at, 3 * CQ :], wu[...]),
        (begin, begin_up, output_ends),
    )
    put_output = local.start(kt, output_ref, False)
    pl.semaphore_wait(credits.at[3], 1)
    rs_pair.take(2)
    rs_pair.begin(0)
    rs_o.last()
    turn_weights(rs_o, wsend)
    net.drain("w1")
    net.drain("mw1")
    net.allow(4, [net.ymate])
    pl.semaphore_wait(credits.at[2], 2)
    rs_q = weight_scatter(
        "w3", gw, sized(wnear, 3 * CQ), sized(wfar, 3 * CQ // 2), wmate.at[pl.ds(0, 3 * CQ)], 3 * CQ
    )
    weight_chunks(rs_q, gw, 0, g_buf)
    rs_in.middle(1)
    rs_in.middle(0)
    rs_u.end(1)
    rs_u.to_mate()
    rs_u.end(0)
    rs_pair.take(1)
    rs_pair.take(3)
    rs_pair.begin_near(0)
    rs_pair.give(0)

    bdp[net.dp] = bsum[...]
    for d in range(1, 8):
        net.send(("b", d), bdp.at[net.dp], bdp.at[net.dp], net.dp_peer(d))
    put_output.wait()
    get_go = local.start(go_in, kt, False)
    rs_pair.middle(0)
    rs_q.middle(1)
    rs_q.middle(0)
    rs_in.end(1)
    rs_in.to_mate()
    rs_in.end(0)
    rs_pair.take(0)
    rs_pair.end(0)
    send_weights(net, "xo", CO, wsend, wrecv_o)
    for d in range(1, 8):
        net.recv(("b", d), bdp.at[lax.rem(net.dp + 8 - d, 8)])
    total = bdp[0]
    for s in range(1, 8):
        total = total + bdp[s]
    bseq[net.seq] = total
    for d in range(1, 8):
        net.send(("c", d), bseq.at[net.seq], bseq.at[net.seq], net.seq_peer(d))
    rs_q.end(1)
    pl.semaphore_wait(credits.at[4], 1)
    rs_q.to_mate()
    rs_q.end(0)
    get_go.wait()
    late = AllSum(net, "f", vec, vseq, vdp, vmate)
    vec[...] = jnp.zeros_like(vec)

    def norm_back(first, scatter=rs_in, start=0):
        at = pl.ds(pl.multiple_of(start + first, 32), 32)
        xhat, rstd = norm_stats(vt[at, :].astype(F32))
        grad, go = scatter.total(first, 32), kt[at, :].astype(F32)
        vec[:, :D] += jnp.sum(grad * xhat, 0, keepdims=True)
        vec[:, D:] += jnp.sum(grad, 0, keepdims=True)
        g = grad * gain_in[...].astype(F32)
        mean_g = jnp.mean(g, -1, keepdims=True)
        mean_gx = jnp.mean(g * xhat, -1, keepdims=True)
        ot[at, :] = go + (g - mean_g - xhat * mean_gx) * rstd

    pieces(32, 32, lambda first: norm_back(first, rs_pair, 96))
    rs_in.last()
    pieces(96, 32, norm_back)
    late.start()
    local.start(ot, ginp_ref)
    receive_weights(net, "xo", wrecv_o)
    local.start(wrecv_o, wo_ref)
    net.drain("xo")
    rs_u.last()
    turn_weights(rs_u, wsend)
    send_weights(net, "xu", CF, wsend, wrecv_u)
    late.second()
    receive_weights(net, "xu", wrecv_u)
    local.start(wrecv_u, wu_ref)
    net.drain("xu")
    rs_q.last()
    turn_weights(rs_q, wsend)
    late.third()
    send_weights(net, "xq", 3 * CQ, wsend, wrecv_q)
    for d in range(1, 8):
        net.recv(("c", d), bseq.at[lax.rem(net.seq + 8 - d, 8)])
    bias_ref[...] = bseq[...]
    sums_ref[...] = late.done()
    receive_weights(net, "xq", wrecv_q)
    local.start(wrecv_q, wq_ref)
    net.drain()
    local.finish()


def any_spec():
    return pl.BlockSpec(memory_space=pl.ANY)


def vmem_spec():
    return pl.BlockSpec(memory_space=pltpu.VMEM)


def struct(shape, dtype):
    return jax.ShapeDtypeStruct(shape, dtype)


def block_call(x, go, qkv, up, att, down, seg, valid, vectors, qkv_b):
    rates = np.tile(10000.0 ** (-2.0 * np.arange(16, dtype=np.float32) / ROT), 8)[None].astype(np.float32)
    scratch = [
        ((T, D), BF), ((T, D), BF), ((4, 256, D), BF), ((D, 3 * CQ), BF), ((D, CF), BF), ((D, CO), BF), ((2, T, 128), F32),
        ((T, 128), F32), ((NQ, 1, 2 * QB), F32), ((NQ, 2 * QB, CQ), BF), ((T, CQ), BF), ((T, CQ), BF), ((CQ, T), BF),
        ((CQ, T), BF), ((T, CI), BF), ((CI, T), BF), ((4, 2, CF, 256), BF), ((CQ, T), F32), ((NQ, 2 * QB, CQ), BF),
        ((T, CQ), F32), ((T, CQ), F32), ((NQ, 1, 2 * QB), F32), ((NQ, 1, 2 * QB), F32),
        ((1, 2 * QB), F32), ((1, 2 * QB), F32), ((CQ, 2 * QB), F32), ((1, CI), F32),
        ((2, 2, 128, D), BF), ((2, 2, 64, D), BF), ((128, D), BF), ((4, 2, CO, 256), BF), ((2, 2, CO, 256), BF),
        ((2, 2, CO // 2, 256), BF), ((CO, 256), BF),
        ((256, CO), BF), ((8, 32, CO), BF), ((8, 32, CF), BF), ((8, 32, 3 * CQ), BF),
        ((1, CS), F32), ((8, 1, CS), F32), ((8, 1, CS), F32), ((1, 2 * D), F32), ((8, 1, 2 * D), F32),
        ((8, 1, 2 * D), F32), ((1, 2 * D), F32),
    ]
    outs = [
        ((T, D), BF), ((128, D), BF), ((128, D), F32), ((1, 2 * D), F32), ((8, 1, CS), F32), ((8, 32, CO), BF),
        ((8, 32, CF), BF), ((8, 32, 3 * CQ), BF),
    ]
    return pl.pallas_call(
        block_kernel,
        out_shape=[struct(*o) for o in outs],
        in_specs=[any_spec()] * 6 + [vmem_spec()] * 5,
        out_specs=[any_spec()] * 3 + [vmem_spec()] * 2 + [any_spec()] * 3,
        scratch_shapes=[pltpu.VMEM(*s) for s in scratch]
        + [pltpu.SemaphoreType.DMA((SLOTS,)), pltpu.SemaphoreType.DMA((SLOTS,)), pltpu.SemaphoreType.DMA((24,))]
        + [pltpu.SemaphoreType.REGULAR((7,))],
        compiler_params=pltpu.CompilerParams(
            collective_id=1, has_side_effects=True, vmem_limit_bytes=VMEM_LIMIT
        ),
        name="block",
    )(x, go, qkv, up, att, down, seg, valid, vectors, qkv_b, jnp.asarray(rates))


def finish_kernel(
    output_in, ginp_in, sums_in, bias_in, wo_in, wu_in, wq_in,
    output_ref, ginp_ref, ggain_ref, gshift_ref, gqkv_ref, gqkvb_ref, gatt_ref, gup_ref, gupb_ref, gdown_ref, gob_ref,
):
    output_ref[...] = output_in[...]
    ginp_ref[...] = ginp_in[...]
    ggain_ref[...] = sums_in[:, :D]
    gshift_ref[...] = sums_in[:, D:]
    for s in range(8):
        out_part, qkv_part, bias_part = wo_in[s].astype(F32), wq_in[s].astype(F32), bias_in[s]
        gatt_ref[:, s * CQ : (s + 1) * CQ] = out_part[:, :CQ]
        gdown_ref[:, s * CF : (s + 1) * CF] = out_part[:, CQ:]
        gup_ref[:, s * CF : (s + 1) * CF] = wu_in[s].astype(F32)
        gupb_ref[:, s * CF : (s + 1) * CF] = bias_part[:, 3 * CQ : CI]
        gob_ref[:, s * 256 : (s + 1) * 256] = bias_part[:, CI:]
        for j in range(3):
            gqkv_ref[j, :, s * CQ : (s + 1) * CQ] = qkv_part[:, j * CQ : (j + 1) * CQ]
            gqkvb_ref[j : j + 1, s * CQ : (s + 1) * CQ] = bias_part[:, j * CQ : (j + 1) * CQ]


def finish_call(output, ginp, sums, bias, wo, wu, wq):
    outs = [
        ((128, D), BF), ((128, D), F32), ((1, D), F32), ((1, D), F32), ((3, 32, 1024), F32), ((3, 1024), F32),
        ((32, 1024), F32), ((32, 4096), F32), ((1, 4096), F32), ((32, 4096), F32), ((1, D), F32),
    ]
    return pl.pallas_call(
        finish_kernel,
        out_shape=[struct(*o) for o in outs],
        in_specs=[vmem_spec()] * 7,
        out_specs=[vmem_spec()] * 11,
        name="finish",
    )(output, ginp, sums, bias, wo, wu, wq)


def shards(
    inputs, segment_ids, valid_mask, norm_gain, norm_bias, qkv_weight, qkv_bias, attn_out_weight, up_weight, up_bias,
    down_weight, out_bias, grad_out,
):
    parts = block_call(
        inputs[0], grad_out[0], jnp.transpose(qkv_weight, (1, 0, 2)), up_weight, attn_out_weight, down_weight, segment_ids,
        valid_mask, jnp.concatenate([norm_gain, norm_bias, out_bias, up_bias])[None], qkv_bias,
    )
    output, ginp, ggain, gshift, gqkv, gqkvb, gatt, gup, gupb, gdown, gob = finish_call(*parts[1:])
    return (
        output[None], ginp[None], ggain[0], gshift[0], jnp.transpose(gqkv, (1, 0, 2)), gqkvb, gatt, gup, gupb[0], gdown, gob[0],
    )


def solution(mesh):
    placed = (
        P("dp", ("seq", "branch"), None), P("dp", None), P("dp", None), P(), P(), P(("dp", "seq"), None, "branch"),
        P(None, "branch"), P(("dp", "seq"), "branch"), P(("dp", "seq"), "branch"), P("branch"),
        P(("dp", "seq"), "branch"), P(), P("dp", ("seq", "branch"), None),
    )
    return jax.shard_map(
        shards,
        mesh=mesh,
        in_specs=placed,
        out_specs=(
            P("dp", ("seq", "branch"), None), P("dp", ("seq", "branch"), None), P(), P(),
            P(("dp", "seq"), None, "branch"), P(None, "branch"), P(("dp", "seq"), "branch"), P(("dp", "seq"), "branch"),
            P("branch"), P(("dp", "seq"), "branch"), P(),
        ),
        check_vma=False,
    )
```

time: 1610 us -> 221 us (0.14)
  waiting for transfers between devices: 1250 us -> 0 us
  Pallas kernels: 0 us -> 215 us
  matrix products: 147 us -> 0 us
  local copies, waits for them, and re-layouts: 137 us -> 0.64 us
  other arithmetic: 47.9 us -> 0.74 us
    reduce_scatter x5 -> x0, waiting for transfers between devices: 466 us -> none  [the longest x1 388 us: shards(): lax.psum_scatter(jnp.einsum('rtn,rtc->nc', columns, grad_entry, preferred...]
    all_gather x6 -> x0, waiting for transfers between devices: 371 us -> none  [the longest x1 169 us: shards(): lax.all_gather(weights_in, ('dp', 'seq'), axis=0, tiled=True)]
    unnamed x14 -> x0, waiting for transfers between devices: 354 us -> none
    pallas_call x0 -> x2, Pallas kernels: none -> 215 us  [the longest x1 212 us: block_call(): pl.pallas_call(block_kernel, out_shape=[struct(*o) for o in outs], in_spe...]
    dot_general x34 -> x0, matrix products: 147 us -> none  [the longest x1 23.1 us: shards(): jnp.einsum('rtn,rtc->nc', columns, grad_entry, preferred_element_type=jnp...]
    unnamed x64 -> x0, local copies, waits for them, and re-layouts: 65.5 us -> none
    psum x1 -> x0, waiting for transfers between devices: 60.3 us -> none  [shards(): lax.psum((slot_terms, grad_gain, grad_shift, out_bias_terms), ('dp', 'seq...]
    reduce_sum x12 -> x0, other arithmetic: 19.9 us -> none  [the longest x4 6.76 us: forward_step(): normaliser = normaliser * fade + jnp.sum(probability, -1)]
  transfers between devices with their start and end apart: 13 -> 0, of which waited for: 12 -> 0; matrix products, arithmetic and copies ran while one was open for 11% -> 0% of each run, Pallas kernels for 0% -> 0%
where the time goes in v1:
time: 221 us; the launch traced here: 217 us
  Pallas kernels  215 us (97%)
    pallas_call x1, Pallas kernels, block_call(): pl.pallas_call(block_kernel, out_shape=[struct(*o) for o in outs], in_spe...  212 us

profile of v1, /device:TPU:24, one launch (start us, length us, event | category | flops | bytes accessed | tf_op | source)
XLA Modules:
  0.0 217.1 jit_solution(1897473859952263232)
XLA Ops:
  0.6 0.7 pad_maximum_fusion
  1.4 0.6 broadcast_in_dim.9.vectors_in
  2.0 211.6 %block.1 = (bf16[2048,2048]{1,0:T(8,128)(2,1)}, bf16[128,2048]{1,0:T(8,128)(2,1)}, f32[128,2048]{1,0:T(8,128)}, f32[1,4096]{1,0:T(1,128)}, f32[8,1,1152]{2,1,0:T...) custom-call(bf16[128,2048]{1,0:T(8,128)(2,1)} %bitcast.10, ...), custom_call_target="tpu_custom_call" | custom-call | tf_op jit(solution)/shard_map/block/pallas_call | solution.py:998
  213.6 3.4 %finish.1 = (bf16[128,2048]{1,0:T(8,128)(2,1)}, f32[128,2048]{1,0:T(8,128)}, f32[1,2048]{1,0:T(1,128)}, f32[1,2048]{1,0:T(1,128)}, f32[3,32,1024]{2,1,0:T(8,128)...) custom-call(bf16[128,2048]{1,0:T(8,128)(2,1)} %get-tuple-element.29., ...), custom_call_target="tpu_custom_call" | custom-call | tf_op jit(solution)/shard_map/finish/pallas_call | solution.py:1038
